TPU v7x, 32 devices: a whole 2x2x4 slice. The times are simulated.
32 devices in a mesh: section: 2 (over core), grp: 4 (over y, x), tile: 4 (over z).
Axes of the slice: x: 2, y: 2, z: 4, core: 2. Of those that a mesh axis runs over, the one named last changes fastest.
Arguments:
- latent: bfloat16 [4, 4, 16, 1536], P('grp', 'section', 'tile'), may hold values from -6 to 6
- latent_mean: float32 [16], replicated, may hold values from -1 to 1
- latent_scale: float32 [16], replicated, may hold values from 0.5 to 3
- cache_latent: bfloat16 [4, 2, 16, 1536], P('grp', None, 'tile', 'section'), may hold values from -9 to 9
- input_weight: bfloat16 [3, 3, 3, 16, 384], replicated, may hold values from -0.3125 to 0.3125
- mid_gain: float32 [384], replicated, may hold values from 0.25 to 1.75
- mid_cache: bfloat16 [4, 2, 16, 96, 384], P('grp', None, 'tile', 'section'), may hold values from -5 to 5
- mid_weight: bfloat16 [3, 3, 3, 384, 384], P(None, None, None, None, 'tile'), may hold values from -0.0625 to 0.0625
- up_weight: bfloat16 [3, 3, 384, 768], replicated, may hold values from -0.109375 to 0.109375
Outputs:
- upsampled: bfloat16 [4, 4, 32, 192, 192], P('grp', None, 'tile', 'section')
All inputs are finite; a program needn't handle non-finite values.
Results may differ from a plain program's by a relative error of at most 0.0064.
Values may be sent and summed in bfloat16 or wider, within the bound.
A program may use at most 128 MiB of HBM per device.

v0:
```python
import functools

import jax
import jax.numpy as jnp
from jax import lax
from jax.experimental import pallas as pl
from jax.experimental.pallas import tpu as pltpu
from jax.sharding import PartitionSpec as P

MESH = pl.DeviceIdType.MESH
PIECES = 8


def exchange_kernel(
    n, w_ref, lat_ref, cl_ref, mc_ref,
    g_ref, latx_ref, clx_ref, mcv_ref, mch_ref,
    own_sem, hs_sem, hr_sem, zs_sem, zr_sem, ps_sem, pr_sem, ss_sem, sr_sem,
):
    s = lax.axis_index("section")
    g = lax.axis_index("grp")
    t = lax.axis_index("tile")
    gx = g + 1 - 2 * (g % 2)
    gy = g + 2 - 4 * ((g // 2) % 2)
    gd = gx + 2 - 4 * ((gx // 2) % 2)
    o = 1 - s
    chunks = w_ref.shape[0]
    per = chunks // PIECES
    half = per // 2
    rest = chunks - per * PIECES
    has = {-1: t > 0, 0: None, 1: t < n - 1}

    def dev(ds=0, group=None, dt=0):
        return {
            "section": o if ds else s,
            "grp": g if group is None else group,
            "tile": t + dt,
        }

    def guarded(cond, fn):
        if cond is None:
            fn()
        else:
            pl.when(cond)(fn)

    partners = [(dev(1), None), (dev(0, gx), None), (dev(0, gy), None)]
    for dt in (-1, 1):
        partners += [(dev(0, None, dt), has[dt]), (dev(1, None, dt), has[dt])]
    barrier = pltpu.get_barrier_semaphore()
    for target, cond in partners:
        guarded(
            cond,
            functools.partial(
                pl.semaphore_signal, barrier, inc=1, device_id=target, device_id_type=MESH
            ),
        )
    own = [
        pltpu.make_async_copy(w_ref, g_ref.at[:, t], own_sem.at[0]),
        pltpu.make_async_copy(lat_ref, latx_ref.at[1, s], own_sem.at[1]),
        pltpu.make_async_copy(cl_ref, clx_ref.at[1, s], own_sem.at[2]),
    ]
    for copy in own:
        copy.start()
    pl.semaphore_wait(barrier, 3 + 2 * (jnp.minimum(t, 1) + jnp.minimum(n - 1 - t, 1)))

    def remote(src, dst, ssem, rsem, target):
        return pltpu.make_async_remote_copy(
            src_ref=src, dst_ref=dst, send_sem=ssem, recv_sem=rsem,
            device_id=target, device_id_type=MESH,
        )

    rows, cols = mc_ref.shape[1], mc_ref.shape[2]
    edge = pl.multiple_of((cols - 16) * o, 16)
    halo = []
    for dt in (-1, 0, 1):
        first = 0 if dt < 0 else rows - 2
        for ds in (0, 1):
            if (ds, dt) == (0, 0):
                continue
            k = len(halo)
            base = 3 * k
            sems = [(hs_sem.at[base + j], hr_sem.at[base + j]) for j in range(3)]
            target = dev(ds, None, dt)
            back = len(halo)
            copies = [
                (lat_ref, latx_ref.at[1 - dt, s]),
                (cl_ref, clx_ref.at[1 - dt, s]),
            ]
            if ds == 0:
                copies.append((mc_ref.at[:, pl.ds(first, 2)], mcv_ref.at[(1 - dt) // 2]))
            elif dt == 0:
                copies.append((mc_ref.at[:, :, pl.ds(edge, 16)], mch_ref.at[1]))
            else:
                copies.append(
                    (
                        mc_ref.at[:, pl.ds(first, 2), pl.ds(edge, 16)],
                        mch_ref.at[1 - dt, :, pl.ds(0, 2)],
                    )
                )
            halo.append(
                (
                    dt,
                    ds,
                    [remote(a, b, x, y, target) for (a, b), (x, y) in zip(copies, sems)],
                )
            )

    events = []
    for i in range(n - 1):
        for d in (0, 1):
            if d == 0:
                events.append((i, d, t - 1 - i, t - 1 - i >= 0))
            else:
                events.append((i, d, t + 1 + i, t + 1 + i <= n - 1))

    def block(group, part, u):
        begin = (2 * (group % 4) + s) * per
        if part == 0:
            return g_ref.at[pl.ds(begin, half), u]
        if part == 1:
            return g_ref.at[pl.ds(begin + half, per - half), u]
        return g_ref.at[pl.ds(begin, per), u]

    tail = pl.ds(per * PIECES, rest)

    def z_copies(i, d, u, first):
        begin = (2 * (g % 4) + s) * per
        dt = 1 if d == 0 else -1
        e = 2 * i + d
        src_a = w_ref.at[pl.ds(begin, per)] if first else block(g, 2, u)
        src_b = w_ref.at[tail] if first else g_ref.at[tail, u]
        target = dev(0, None, dt)
        return [
            remote(src_a, block(g, 2, u), zs_sem.at[2 * e], zr_sem.at[2 * e], target),
            remote(src_b, g_ref.at[tail, u], zs_sem.at[2 * e + 1], zr_sem.at[2 * e + 1], target),
        ]

    def d_copies(e, u):
        def one(k, group, part, to):
            b = block(group, part, u)
            return remote(b, b, ps_sem.at[6 * e + k], pr_sem.at[6 * e + k], dev(0, to))

        first = [one(0, g, 0, gx), one(1, g, 1, gy)]
        second = [one(2, g, 0, gy), one(3, gx, 0, gy), one(4, g, 1, gx), one(5, gy, 1, gx)]
        return first, second

    def s_copies(e, u):
        plan = [(g, 2), (gx, 0), (gy, 1), (gy, 0), (gd, 0), (gx, 1), (gd, 1)]
        made = []
        for k, (group, part) in enumerate(plan):
            b = block(group, part, u)
            made.append(remote(b, b, ss_sem.at[7 * e + k], sr_sem.at[7 * e + k], dev(1)))
        return made

    def begin_z(i, d, u, valid, first):
        dt = 1 if d == 0 else -1

        def go():
            for copy in z_copies(i, d, u, first):
                copy.start()

        pl.when(jnp.logical_and(valid, has[dt]))(go)

    def end_z(i, d, u, valid):
        dt = 1 if d == 0 else -1

        def go():
            for copy in z_copies(i, d, u, i == 0):
                copy.wait_send()

        pl.when(jnp.logical_and(valid, has[dt]))(go)

    begin_z(0, 0, t, t >= 0, True)
    begin_z(0, 1, t, t >= 0, True)
    for dt, ds, copies in halo:
        def go(copies=copies):
            for copy in copies:
                copy.start()
        guarded(has[dt], go)

    def arrive(e, i, d, u):
        for copy in z_copies(i, d, u, False):
            copy.wait_recv()

    def stage_a(i, d, u, valid):
        e = 2 * i + d

        def go():
            arrive(e, i, d, u)
            for copy in d_copies(e, u)[0]:
                copy.start()
            s_copies(e, u)[0].start()

        pl.when(valid)(go)
        if i + 1 < n - 1:
            begin_z(i + 1, d, u, valid, False)

    def stage_b(i, d, u, valid):
        e = 2 * i + d

        def go():
            first, second = d_copies(e, u)
            sib = s_copies(e, u)
            first[0].wait_recv()
            second[0].start()
            second[1].start()
            sib[1].start()
            first[1].wait_recv()
            second[2].start()
            second[3].start()
            sib[2].start()

        pl.when(valid)(go)

    def stage_c(i, d, u, valid):
        e = 2 * i + d

        def go():
            _, second = d_copies(e, u)
            sib = s_copies(e, u)
            for k in range(4):
                second[k].wait_recv()
                sib[3 + k].start()

        pl.when(valid)(go)

    for slot in range(n + 1):
        for stage, lag in ((stage_a, 0), (stage_b, 1), (stage_c, 2)):
            i = slot - lag
            if 0 <= i < n - 1:
                for event in events[2 * i : 2 * i + 2]:
                    stage(*event)

    for copy in own:
        copy.wait()
    for dt, ds, copies in halo:
        guarded(has[dt], lambda copies=copies: [c.wait_send() for c in copies] and None)
    order = {(dt, ds): copies for dt, ds, copies in halo}
    for (dt, ds), copies in order.items():
        guarded(has[-dt], lambda copies=copies: [c.wait_recv() for c in copies] and None)
    for i, d, u, valid in events:
        e = 2 * i + d

        def finish(e=e, u=u):
            first, second = d_copies(e, u)
            for copy in first + second:
                copy.wait_send()
            for copy in s_copies(e, u):
                copy.wait()

        pl.when(valid)(finish)
        sent = t - i if d == 0 else t + i
        end_z(i, d, sent, sent >= 0 if d == 0 else sent <= n - 1)


def exchange(n, weights, latent, cache_latent, mid_cache):
    chunks, cw, lanes = weights.shape
    frames, rows, cols, channels = mid_cache.shape
    dt = weights.dtype
    shape = jax.ShapeDtypeStruct
    events = 2 * (n - 1)
    dma = lambda k: pltpu.SemaphoreType.DMA((k,))
    return pl.pallas_call(
        functools.partial(exchange_kernel, n),
        out_shape=(
            shape((chunks, n, cw, lanes), dt),
            shape((3, 2) + latent.shape, dt),
            shape((3, 2) + cache_latent.shape, dt),
            shape((2, frames, 2, cols, channels), dt),
            shape((3, frames, rows, 16, channels), dt),
        ),
        in_specs=[pl.BlockSpec(memory_space=pl.ANY)] * 4,
        out_specs=[pl.BlockSpec(memory_space=pl.ANY)] * 5,
        scratch_shapes=[
            dma(3), dma(15), dma(15), dma(2 * events), dma(2 * events),
            dma(6 * events), dma(6 * events), dma(7 * events), dma(7 * events),
        ],
        compiler_params=pltpu.CompilerParams(collective_id=0, has_side_effects=True),
    )(weights, latent, cache_latent, mid_cache)


def activate(values, gain_vector):
    floats = values.astype(jnp.float32)
    inverse_rms = lax.rsqrt(jnp.mean(floats * floats, axis=-1, keepdims=True) + 1e-06)
    return jax.nn.silu(floats * inverse_rms * gain_vector).astype(jnp.bfloat16)


def to_pixels(phases, out_channels):
    frame_count, row_count, col_count, _ = phases.shape
    split = phases.reshape(frame_count, row_count, col_count, 2, 2, out_channels)
    return jnp.transpose(split, (0, 1, 3, 2, 4, 5)).reshape(
        frame_count, 2 * row_count, 2 * col_count, out_channels
    )


def inside(start, count, limit):
    index = start + jnp.arange(count)
    return jnp.logical_and(index >= 0, index < limit)


def mid_conv(stacked, weights):
    kernel = weights.reshape(3, 3, 3, 3, -1, weights.shape[-1])
    kernel = jnp.transpose(kernel, (0, 1, 2, 3, 5, 4))
    kernel = kernel.reshape(3, 3, 3, -1, kernel.shape[-1])
    return lax.conv_general_dilated(
        stacked[None], kernel, (1, 1, 1), [(0, 0)] * 3,
        dimension_numbers=("NDHWC", "DHWIO", "NDHWC"),
        preferred_element_type=jnp.float32,
    )[0]


def local(
    n, latent, latent_mean, latent_scale, cache_latent, input_weight,
    mid_gain, mid_cache, mid_weight, up_weight,
):
    s = lax.axis_index("section")
    t = lax.axis_index("tile")
    channels = latent_mean.shape[0]
    mid = input_weight.shape[-1]
    cw = mid_weight.shape[-1]
    lanes = 128
    _, rows, cols, _ = mid_cache.shape[1:]
    shard = mid_weight.reshape(-1, lanes, cw).transpose(0, 2, 1)
    gathered, latx, clx, mcv, mch = exchange(
        n, shard, latent[0], cache_latent[0], mid_cache[0]
    )
    width = latx.shape[-1]
    frames = 2 * latx.shape[2]
    near = latx.transpose(1, 2, 0, 3, 4).reshape(frames, 3 * rows, width)[:, rows - 3 : 2 * rows + 3]
    repeats = width // channels
    scaled = (
        near.astype(jnp.float32) * jnp.tile(latent_scale, repeats) + jnp.tile(latent_mean, repeats)
    ).astype(jnp.bfloat16)
    cached = clx.transpose(2, 0, 3, 1, 4).reshape(clx.shape[2], 3 * rows, width)
    cached = cached[:, rows - 3 : 2 * rows + 3]
    joined = jnp.concatenate([cached, scaled], axis=0)
    joined = jnp.where(inside(t * rows - 3, rows + 6, n * rows)[:, None], joined, 0)
    joined = jnp.pad(joined, ((0, 0), (0, 0), (3 * channels, 3 * channels)))
    joined = lax.dynamic_slice_in_dim(joined, s * cols * channels, (cols + 6) * channels, axis=2)
    joined = joined.reshape(joined.shape[0], rows + 6, cols + 6, channels)
    features = lax.conv_general_dilated(
        joined[None], input_weight, (1, 1, 1), [(0, 0)] * 3,
        dimension_numbers=("NDHWC", "DHWIO", "NDHWC"),
        preferred_element_type=jnp.float32,
    )[0].astype(jnp.bfloat16)
    sided = jnp.concatenate([mch[0, :, :2], mch[1], mch[2, :, :2]], axis=1)
    sided = lax.dynamic_slice_in_dim(sided, 14 * s, 2, axis=2)
    centre = jnp.concatenate([mcv[0], mid_cache[0], mcv[1]], axis=1)
    cache = jnp.concatenate([sided, centre, sided], axis=2)
    stacked = jnp.concatenate([cache, activate(features, mid_gain)], axis=0)
    row_ok = inside(t * rows - 2, rows + 4, n * rows)[:, None, None]
    col_ok = inside(s * cols - 2, cols + 4, 2 * cols)[:, None]
    stacked = jnp.where(jnp.logical_and(row_ok, col_ok), stacked, 0)
    branch = mid_conv(stacked, gathered.reshape(gathered.shape[0], mid, lanes))
    mixed = features[:, 1:-1, 1:-1].astype(jnp.float32) + branch
    keep = jnp.logical_and(row_ok, col_ok)[1:-1, 1:-1]
    mixed = jnp.where(keep, mixed, 0).astype(jnp.bfloat16)
    phases = lax.conv_general_dilated(
        mixed, up_weight, (1, 1), [(0, 0), (0, 0)],
        dimension_numbers=("NHWC", "HWIO", "NHWC"),
        preferred_element_type=jnp.float32,
    ).astype(jnp.bfloat16)
    return to_pixels(phases, up_weight.shape[3] // 4)[None]


def solution(mesh):
    return jax.shard_map(
        functools.partial(local, mesh.shape["tile"]),
        mesh=mesh,
        in_specs=(
            P("grp", "section", "tile", None),
            P(),
            P(),
            P("grp", None, "tile", "section"),
            P(),
            P(),
            P("grp", None, "tile", "section", None),
            P(None, None, None, None, "tile"),
            P(),
        ),
        out_specs=P("grp", None, "tile", "section", None),
        check_vma=False,
    )
```

profile of v0, /device:TPU:12, one launch (start us, length us, event | category | flops | bytes accessed | tf_op | source)
XLA Modules:
  0.0 150.7 jit_solution(5712107592669235179)
XLA Ops:
  0.0 3.0 %copy.77 = bf16[3,3,3,384,96]{3,2,1,0,4:T(4,128)(2,1)S(1)} copy(bf16[3,3,3,384,96]{3,4,2,1,0:T(8,128)(2,1)} %param.16) | data formatting | bytes 3981312 | tf_op args[7]
  3.0 3.5 %reshape.127 = bf16[81,128,96]{1,0,2:T(8,128)(2,1)} reshape(bf16[3,3,3,384,96]{3,2,1,0,4:T(4,128)(2,1)S(1)} %copy.77) | data formatting | bytes 3981312 | tf_op jit(solution)/shard_map/reshape | solution.py:322
  6.4 3.2 %copy.118 = bf16[81,128,96]{1,2,0:T(8,128)(2,1)} copy(bf16[81,128,96]{1,0,2:T(8,128)(2,1)} %reshape.127) | data formatting | bytes 3981312 | tf_op jit(solution)/shard_map/reshape | solution.py:322
  9.6 64.7 %shard_map.91 = (bf16[81,4,96,128]{3,2,1,0:T(8,128)(2,1)}, bf16[3,2,2,4,1536]{4,3,2,1,0:T(4,128)(2,1)}, bf16[3,2,2,4,768]{4,3,2,1,0:T(4,128)(2,1)}, bf16[2,2,2,4...) custom-call(bf16[81,96,128]{2,1,0:T(8,128)(2,1)} %bitcast.94, bf16[2,4,1536]{2,1,0:T(4,128)(2,1)} %bitcast.105, ...), custom_call_target="tpu_custom_call" | custom-call | tf_op jit(solution)/shard_map/pallas_call | solution.py:262
  74.3 0.0 copy-start.4
  74.3 0.0 copy-start.7
  74.3 0.0 copy-start.8
  74.3 15.2 %copy.91 = bf16[3,3,3,3,128,384]{5,4,3,2,1,0:T(8,128)(2,1)} copy(bf16[3,3,3,3,128,384]{4,5,3,2,1,0:T(8,128)(2,1)} %bitcast.93) | data formatting | bytes 15925248 | tf_op jit(solution)/shard_map/transpose | solution.py:302
  89.5 0.1 copy.80
  89.6 0.1 reshape.129
  89.7 0.1 add.72
  89.8 0.1 mul.49
  89.9 0.1 add_convert_fusion
  90.0 0.1 copy.79
  90.0 0.1 reshape.128
  90.2 0.1 maximum_select_fusion.1
  90.3 0.1 pad_dynamic-slice_fusion
  90.4 0.6 reshape.155
  91.1 0.2 pad.5
  91.3 0.0 copy-start.11
  91.3 0.3 reshape.175
  91.6 0.1 copy.83
  91.7 0.1 slice.48
  91.8 0.1 copy-done.11
  91.9 1.9 %select_convert_fusion.1 = bf16[4,8,8,7,384]{4,2,3,1,0:T(8,128)(2,1)S(1)} fusion(bf16[3,3,3,16,384]{4,3,2,1,0:T(8,128)(2,1)S(1)} %copy-done, pred[8,7]{0,1:T(8,128)(4,1)S(1)} %copy-done.11, bf16[6,10,1,7,2,16]{5,3,4,1,0,2:T(8,128)(2,1)S(1)} %slice.48, bf16[6,10,1,8,7,16]{5,3,4,1,0,2:T(8,128)(2,1)S(1)} %copy.83), kind=kOutput, calls=%fused_computation.3 | convolution fusion | flops 596333568 | bytes 1842488 | tf_op jit(solution)/shard_map/conv_general_dilated | solution.py:340
  93.8 1.8 %copy.85 = f32[4,8,8,7,384]{4,1,3,2,0:T(8,128)} copy(bf16[4,8,8,7,384]{4,2,3,1,0:T(8,128)(2,1)S(1)} %select_convert_fusion.1) | data formatting | bytes 4128768 | tf_op jit(solution)/shard_map/convert_element_type | solution.py:282
  95.7 0.2 copy.84
  95.9 0.3 multiply_reduce_fusion
  96.2 0.1 copy.86
  96.3 0.1 copy.87
  96.4 0.0 copy-start.2
  96.4 2.5 %multiply_convert_fusion = bf16[1,4,8,52,384]{4,2,3,1,0:T(8,128)(2,1)S(1)} fusion(f32[4,8,1,56,384]{4,1,3,0,2:T(8,128)} %bitcast.90, f32[4,8,52]{1,2,0:T(8,128)S(1)} %copy.87, f32[384]{0:T(512)S(1)} %copy-done.6), kind=kLoop, calls=%fused_computation.15 | loop fusion | flops 4472832 | bytes 3842048 | tf_op jit(solution)/shard_map/convert_element_type | solution.py:284
  99.0 0.8 slice_bitcast_fusion.6
  99.8 0.9 slice_bitcast_fusion.4
  100.8 0.3 maximum_bitcast_fusion
  101.1 0.9 copy.88
  102.1 0.1 broadcast_and_fusion
  102.2 1.4 fusion.15
  103.6 0.2 pad.7
  103.8 0.0 copy-start.10
  103.8 0.3 copy.90
  104.1 0.1 slice.52
  104.2 0.2 copy-done.10
  104.5 24.9 %fusion.16 = f32[4,6,8,7,384]{4,2,3,1,0:T(8,128)S(1)} fusion(bf16[3,3,3,384,384]{4,3,2,1,0:T(8,128)(2,1)} %bitcast.92, bf16[6,8,1,7,2,384]{5,3,4,1,0,2:T(8,128)(2,1)S(1)} %slice.52, bf16[6,8,1,8,7,384]{5,3,4,1,0,2:T(8,128)(2,1)S(1)} %copy.90, pred[8,7]{0,1:T(8,128)(4,1)S(1)} %copy-done.10), kind=kOutput, calls=%fused_computation.26 | convolution fusion | flops 10710245376 | bytes 12607544 | tf_op jit(solution)/shard_map/conv_general_dilated | solution.py:304
  129.3 0.8 copy.92
  130.2 0.3 slice.53
  130.5 1.2 slice_bitcast_fusion
  131.7 0.1 broadcast_and_fusion.1
  131.7 0.1 slice_bitcast_fusion.7
  131.8 0.1 copy.76
  131.9 2.0 %fusion.23 = bf16[6,4,50,384]{3,0,2,1:T(8,128)(2,1)S(1)} fusion(f32[4,6,1,50,384]{4,0,3,1,2:T(4,128)S(1)} %slice.53, bf16[4,8,52,384]{3,1,2,0:T(8,128)(2,1)} %slice_bitcast_fusion, pred[6,50]{0,1:T(8,128)(4,1)S(1)} %copy.76), kind=kLoop, calls=%fused_computation.32 | loop fusion | flops 1843200 | bytes 3686700 | tf_op jit(solution)/shard_map/convert_element_type | solution.py:356
  134.0 0.4 copy.103
  134.3 0.0 copy-start.9
  134.3 0.4 pad.9.clone
  134.7 0.1 slice.54
  134.8 0.6 fusion.19
  135.4 8.9 %select_convert_fusion = bf16[4,32,7,768]{3,1,2,0:T(8,128)(2,1)S(1)} fusion(bf16[3,3,384,768]{3,2,1,0:T(8,128)(2,1)} %param.17, pred[32,7]{0,1:T(8,128)(4,1)S(1)} %copy-done.9, bf16[6,4,8,9,384]{4,1,3,2,0:T(4,128)(2,1)S(1)} %fusion.19), kind=kOutput, calls=%fused_computation.2 | convolution fusion | flops 4757716992 | bytes 8012000 | tf_op jit(solution)/shard_map/conv_general_dilated | solution.py:357
  144.3 1.1 copy.96
  145.3 0.4 slice_bitcast_fusion.1
  145.7 0.1 copy.97
  145.9 1.3 reshape.131
  147.2 0.0 copy-start.1
  147.2 2.0 %copy.98 = bf16[4,4,2,48,2,192]{5,0,4,3,2,1:T(4,128)(2,1)S(1)} copy(bf16[4,4,2,48,2,192]{5,4,2,3,1,0:T(2,128)(2,1)S(1)} %bitcast.97) | data formatting | bytes 2359296 | tf_op jit(solution)/shard_map/transpose | solution.py:290
  149.2 1.4 copy.99
  (23 shorter events, 0.2 us)
Async XLA Ops:
  0.0 91.8 %copy-start = (bf16[3,3,3,16,384]{4,3,2,1,0:T(8,128)(2,1)S(1)}, bf16[3,3,3,16,384]{4,3,2,1,0:T(8,128)(2,1)}, u32[]{:S(2)}) copy-start(bf16[3,3,3,16,384]{4,3,2,1,0:T(8,128)(2,1)} %param.13) | copy-start | bytes 995332
  74.3 15.2 %copy-start.4 = (bf16[3,2,2,4,1536]{4,3,2,1,0:T(4,128)(2,1)S(1)}, bf16[3,2,2,4,1536]{4,3,2,1,0:T(4,128)(2,1)}, u32[]{:S(2)}) copy-start(bf16[3,2,2,4,1536]{4,3,2,1,0:T(4,128)(2,1)} %get-tuple-element.11) | copy-start | bytes 442372
  74.3 15.4 %copy-start.7 = (f32[16]{0:T(128)S(1)}, f32[16]{0:T(128)}, u32[]{:S(2)}) copy-start(f32[16]{0:T(128)} %param.10) | copy-start | bytes 196
  74.3 15.5 %copy-start.8 = (f32[16]{0:T(128)S(1)}, f32[16]{0:T(128)}, u32[]{:S(2)}) copy-start(f32[16]{0:T(128)} %param.11) | copy-start | bytes 196
  74.3 15.6 %copy-start.5 = (bf16[3,2,2,4,768]{4,3,2,1,0:T(4,128)(2,1)S(1)}, bf16[3,2,2,4,768]{4,3,2,1,0:T(4,128)(2,1)}, u32[]{:S(2)}) copy-start(bf16[3,2,2,4,768]{4,3,2,1,0:T(4,128)(2,1)} %get-tuple-element.10) | copy-start | bytes 221188
  91.3 0.7 copy-start.11
  95.7 0.7 copy-start.6
  96.4 4.4 %copy-start.3 = (bf16[2,2,2,48,384]{4,3,2,1,0:T(8,128)(2,1)S(1)}, bf16[2,2,2,48,384]{4,3,2,1,0:T(8,128)(2,1)}, u32[]{:S(2)}) copy-start(bf16[2,2,2,48,384]{4,3,2,1,0:T(8,128)(2,1)} %get-tuple-element.13) | copy-start | bytes 884740
  96.4 4.4 %copy-start.2 = (bf16[1,2,4,48,384]{4,3,2,1,0:T(8,128)(2,1)S(1)}, bf16[1,2,4,48,384]{4,3,2,1,0:T(8,128)(2,1)}, u32[]{:S(2)}) copy-start(bf16[1,2,4,48,384]{4,3,2,1,0:T(8,128)(2,1)} %param.15) | copy-start | bytes 884740
  103.8 0.7 copy-start.10
  134.3 1.1 copy-start.9
  147.2 3.5 %copy-start.1 = (bf16[3,3,3,16,384]{4,3,2,1,0:T(8,128)(2,1)S(1)}, bf16[3,3,3,16,384]{4,3,2,1,0:T(8,128)(2,1)}, u32[]{:S(2)}) copy-start(bf16[3,3,3,16,384]{4,3,2,1,0:T(8,128)(2,1)} %param.13) | copy-start | bytes 995332
where the time goes:
time: 151 us
  Pallas kernels  64.7 us (43%)
  local copies, waits for them, and re-layouts  42.3 us (28%)
  matrix products  35.6 us (24%)
  other arithmetic  7.59 us (5%)
    pallas_call x1, Pallas kernels, exchange(): pl.pallas_call(functools.partial(exchange_kernel, n), out_shape=(shape((c...  64.7 us
    conv_general_dilated x1, matrix products, mid_conv(): lax.conv_general_dilated(stacked[None], kernel, (1, 1, 1), [(0, 0)] * 3,...  24.9 us
    transpose x1, local copies, waits for them, and re-layouts, mid_conv(): kernel = jnp.transpose(kernel, (0, 1, 2, 3, 5, 4))  15.2 us
    conv_general_dilated x1, matrix products, local(): lax.conv_general_dilated(mixed, up_weight, (1, 1), [(0, 0), (0, 0)], dime...  8.86 us
    reshape x2, local copies, waits for them, and re-layouts, local(): shard = mid_weight.reshape(-1, lanes, cw).transpose(0, 2, 1)  6.65 us
    unnamed x26, local copies, waits for them, and re-layouts  3.73 us

commit v1 on v0

--- a/solution.py
+++ b/solution.py
@@ -284,28 +284,118 @@
     return jax.nn.silu(floats * inverse_rms * gain_vector).astype(jnp.bfloat16)
 
 
-def to_pixels(phases, out_channels):
-    frame_count, row_count, col_count, _ = phases.shape
-    split = phases.reshape(frame_count, row_count, col_count, 2, 2, out_channels)
-    return jnp.transpose(split, (0, 1, 3, 2, 4, 5)).reshape(
-        frame_count, 2 * row_count, 2 * col_count, out_channels
-    )
-
-
 def inside(start, count, limit):
     index = start + jnp.arange(count)
     return jnp.logical_and(index >= 0, index < limit)
 
 
-def mid_conv(stacked, weights):
-    kernel = weights.reshape(3, 3, 3, 3, -1, weights.shape[-1])
-    kernel = jnp.transpose(kernel, (0, 1, 2, 3, 5, 4))
-    kernel = kernel.reshape(3, 3, 3, -1, kernel.shape[-1])
-    return lax.conv_general_dilated(
-        stacked[None], kernel, (1, 1, 1), [(0, 0)] * 3,
-        dimension_numbers=("NDHWC", "DHWIO", "NDHWC"),
-        preferred_element_type=jnp.float32,
-    )[0]
+def convs_kernel(
+    x_ref, feat_ref, mask_ref, w_ref, u_ref, out_ref, xs_ref, acc_ref, mx_ref, up_ref, tmp_ref
+):
+    step = pl.program_id(0)
+    total, tall, wide, mid = x_ref.shape
+    frames, inner = total - 2, tall - 2
+    rows = inner - 2
+    cols = out_ref.shape[2] // 2
+    out_channels = out_ref.shape[3]
+    pair = 2
+
+    @pl.when(step == 0)
+    def _():
+        acc_ref[...] = jnp.zeros_like(acc_ref)
+
+        @pl.loop(0, total)
+        def _(f):
+            value = x_ref[f].reshape(tall * wide, mid).astype(jnp.float32)
+            for c in (1, 2):
+                moved = pltpu.roll(value, tall * wide - c, axis=0)
+                xs_ref[c - 1, f] = moved.astype(jnp.bfloat16).reshape(tall, wide, mid)
+
+    @pl.when(step < 9)
+    def _():
+        a, b = step // 3, step % 3
+        for c in range(3):
+            weights = jnp.concatenate([w_ref[3 * c + k] for k in range(3)], axis=1)
+            for p in range(frames // pair):
+                where = (pl.ds(a + pair * p, pair), pl.ds(b, inner))
+                left = x_ref[where] if c == 0 else xs_ref[(c - 1,) + where]
+                size = pair * inner * wide
+                acc_ref[p * size : (p + 1) * size] += lax.dot_general(
+                    left.reshape(size, mid), weights, (((1,), (1,)), ((), ())),
+                    preferred_element_type=jnp.float32,
+                )
+
+    @pl.when(step == 9)
+    def _():
+        up_ref[...] = jnp.zeros_like(up_ref)
+        size = inner * wide
+
+        @pl.loop(0, frames)
+        def _(f):
+            at = pl.ds(pl.multiple_of(f * size, size), size)
+            value = acc_ref[at] + feat_ref[f].reshape(size, mid).astype(jnp.float32)
+            value = jnp.where(mask_ref[...] > 0, value, 0.0)
+            for c in range(3):
+                moved = value if c == 0 else pltpu.roll(value, size - c, axis=0)
+                mx_ref[c, f] = moved.astype(jnp.bfloat16).reshape(inner, wide, mid)
+
+    @pl.when(step >= 9)
+    def _():
+        b = step - 9
+        for c in range(3):
+            for p in range(frames // pair):
+                left = mx_ref[c, pl.ds(pair * p, pair), pl.ds(b, rows), pl.ds(0, cols)]
+                size = pair * rows * cols
+                up_ref[p * size : (p + 1) * size] += jnp.dot(
+                    left.reshape(size, mid), u_ref[c], preferred_element_type=jnp.float32
+                )
+
+    @pl.when(step == 11)
+    def _():
+        @pl.loop(0, frames * rows)
+        def _(q):
+            f, r = q // rows, q % rows
+            value = up_ref[pl.ds(pl.multiple_of(q * cols, cols), cols)]
+            value = jnp.concatenate([value, jnp.zeros((cols, 128), jnp.float32)], axis=1)
+            for i in range(2):
+                for j in range(2):
+                    k = (2 * i + j) * out_channels
+                    for h in range(tmp_ref.shape[0]):
+                        part = value[:, k + 128 * h : k + 128 * h + 128]
+                        tmp_ref[h, pl.ds(j, cols, stride=2), :] = part
+                joined = jnp.concatenate([tmp_ref[h] for h in range(tmp_ref.shape[0])], axis=1)
+                out_ref[f, 2 * r + i] = joined[:, :out_channels].astype(jnp.bfloat16)
+
+
+def convs(stacked, features, mask, weights, up_weight, cols):
+    total, tall, wide, mid = stacked.shape
+    frames, inner = total - 2, tall - 2
+    rows = inner - 2
+    phases = up_weight.shape[-1]
+    whole = pl.BlockSpec(memory_space=pltpu.VMEM)
+    flops = 2 * frames * wide * inner * 27 * mid * mid
+    return pl.pallas_call(
+        convs_kernel,
+        grid=(12,),
+        out_shape=jax.ShapeDtypeStruct((frames, 2 * rows, 2 * cols, phases // 4), jnp.bfloat16),
+        in_specs=[
+            whole,
+            whole,
+            whole,
+            pl.BlockSpec((9, mid, weights.shape[2]), lambda i: (jnp.minimum(i, 8), 0, 0)),
+            pl.BlockSpec((3, mid, phases), lambda i: (jnp.maximum(i - 9, 0), 0, 0)),
+        ],
+        out_specs=whole,
+        scratch_shapes=[
+            pltpu.VMEM((2, total, tall, wide, mid), jnp.bfloat16),
+            pltpu.VMEM((frames * inner * wide, mid), jnp.float32),
+            pltpu.VMEM((3, frames, inner, wide, mid), jnp.bfloat16),
+            pltpu.VMEM((frames * rows * cols, phases), jnp.float32),
+            pltpu.VMEM((-(-phases // 512), 2 * cols, 128), jnp.float32),
+        ],
+        compiler_params=pltpu.CompilerParams(vmem_limit_bytes=48 * 2**20),
+        cost_estimate=pl.CostEstimate(flops=flops, bytes_accessed=16 * 2**20, transcendentals=0),
+    )(stacked, features, mask, weights, up_weight)
 
 
 def local(
@@ -350,16 +440,16 @@
     row_ok = inside(t * rows - 2, rows + 4, n * rows)[:, None, None]
     col_ok = inside(s * cols - 2, cols + 4, 2 * cols)[:, None]
     stacked = jnp.where(jnp.logical_and(row_ok, col_ok), stacked, 0)
-    branch = mid_conv(stacked, gathered.reshape(gathered.shape[0], mid, lanes))
-    mixed = features[:, 1:-1, 1:-1].astype(jnp.float32) + branch
-    keep = jnp.logical_and(row_ok, col_ok)[1:-1, 1:-1]
-    mixed = jnp.where(keep, mixed, 0).astype(jnp.bfloat16)
-    phases = lax.conv_general_dilated(
-        mixed, up_weight, (1, 1), [(0, 0), (0, 0)],
-        dimension_numbers=("NHWC", "HWIO", "NHWC"),
-        preferred_element_type=jnp.float32,
-    ).astype(jnp.bfloat16)
-    return to_pixels(phases, up_weight.shape[3] // 4)[None]
+    wide = -(-(cols + 4) // 16) * 16
+    stacked = jnp.pad(stacked, ((0, 0), (0, 0), (0, wide - cols - 4), (0, 0)))
+    inner = jnp.pad(features[:, 1:-1, 1:], ((0, 0), (0, 0), (0, wide - cols - 3), (0, 0)))
+    keep = jnp.logical_and(row_ok, col_ok)[1:-1, 1:]
+    keep = jnp.pad(keep, ((0, 0), (0, wide - cols - 3), (0, 0))).astype(jnp.float32)
+    out = convs(
+        stacked, inner, keep.reshape(-1, 1), gathered.reshape(gathered.shape[0], mid, lanes),
+        up_weight.reshape((9,) + up_weight.shape[2:]), cols,
+    )
+    return out[None]
 
 
 def solution(mesh):

time: 151 us -> 131 us (0.87)
  Pallas kernels: 64.7 us -> 100 us
  matrix products: 35.6 us -> 8.79 us
  local copies, waits for them, and re-layouts: 42.3 us -> 17.9 us
  other arithmetic: 7.59 us -> 3.12 us
    pallas_call x0 -> x1, Pallas kernels: none -> 35.4 us  [convs(): pl.pallas_call(convs_kernel, grid=(12,), out_shape=jax.ShapeDtypeStruct((...]
    conv_general_dilated x2 -> x0, matrix products: 33.7 us -> none  [the longest x1 24.9 us: mid_conv(): lax.conv_general_dilated(stacked[None], kernel, (1, 1, 1), [(0, 0)] * 3,...]
    transpose x2 -> x0, local copies, waits for them, and re-layouts: 17.2 us -> none  [the longest x1 15.2 us: mid_conv(): kernel = jnp.transpose(kernel, (0, 1, 2, 3, 5, 4))]
    conv_general_dilated x1, matrix products: 1.9 us -> 8.79 us  [local(): lax.conv_general_dilated(joined[None], input_weight, (1, 1, 1), [(0, 0)]...]
    convert_element_type x7 -> x0, local copies, waits for them, and re-layouts: 5.15 us -> none  [the longest x1 1.84 us: activate(): floats = values.astype(jnp.float32)]
    conv_general_dilated x8 -> x0, local copies, waits for them, and re-layouts: 2.16 us -> none  [the longest x4 1.54 us: mid_conv(): lax.conv_general_dilated(stacked[None], kernel, (1, 1, 1), [(0, 0)] * 3,...]
    convert_element_type x1 -> x0, other arithmetic: 2.01 us -> none  [local(): mixed = jnp.where(keep, mixed, 0).astype(jnp.bfloat16)]
    convert_element_type x1, other arithmetic: 2.52 us -> 0.85 us  [activate(): return jax.nn.silu(floats * inverse_rms * gain_vector).astype(jnp.bfloat16)]
where the time goes in v1:
time: 131 us; the launch traced here: 130 us
  Pallas kernels  100 us (76%)
  local copies, waits for them, and re-layouts  17.9 us (14%)
  matrix products  8.79 us (7%)
  other arithmetic  3.12 us (2%)
    pallas_call x1, Pallas kernels, exchange(): pl.pallas_call(functools.partial(exchange_kernel, n), out_shape=(shape((c...  64.7 us
    pallas_call x1, Pallas kernels, convs(): pl.pallas_call(convs_kernel, grid=(12,), out_shape=jax.ShapeDtypeStruct((...  35.4 us
    conv_general_dilated x1, matrix products, local(): lax.conv_general_dilated(joined[None], input_weight, (1, 1, 1), [(0, 0)]...  8.79 us
    reshape x2, local copies, waits for them, and re-layouts, local(): shard = mid_weight.reshape(-1, lanes, cw).transpose(0, 2, 1)  6.7 us
    unnamed x7, local copies, waits for them, and re-layouts  2.94 us

profile of v1, /device:TPU:12, one launch (start us, length us, event | category | flops | bytes accessed | tf_op | source)
XLA Modules:
  0.0 130.1 jit_solution(7657054030422599622)
XLA Ops:
  0.0 0.0 copy-start
  0.0 0.1 broadcast_and_fusion
  0.1 0.1 broadcast_and_fusion.1
  0.2 0.1 slice.35
  0.3 0.7 tile.5
  0.9 0.1 add.73
  1.0 0.7 tile.4
  1.7 0.1 mul.46
  1.8 0.2 reshape.114.mask_ref
  1.9 2.9 %copy.11 = bf16[3,3,3,384,96]{3,2,1,0,4:T(4,128)(2,1)S(1)} copy(bf16[3,3,3,384,96]{3,4,2,1,0:T(8,128)(2,1)} %param.16) | data formatting | bytes 3981312 | tf_op args[7]
  4.9 3.4 %reshape.105 = bf16[81,128,96]{1,0,2:T(8,128)(2,1)} reshape(bf16[3,3,3,384,96]{3,2,1,0,4:T(4,128)(2,1)S(1)} %copy.11) | data formatting | bytes 3981312 | tf_op jit(solution)/shard_map/reshape | solution.py:412
  8.3 3.3 %copy.25 = bf16[81,128,96]{1,2,0:T(8,128)(2,1)} copy(bf16[81,128,96]{1,0,2:T(8,128)(2,1)} %reshape.105) | data formatting | bytes 3981312 | tf_op jit(solution)/shard_map/reshape | solution.py:412
  11.6 64.7 %shard_map.91 = (bf16[81,4,96,128]{3,2,1,0:T(8,128)(2,1)}, bf16[3,2,2,4,1536]{4,3,2,1,0:T(4,128)(2,1)}, bf16[3,2,2,4,768]{4,3,2,1,0:T(4,128)(2,1)}, bf16[2,2,2,4...) custom-call(bf16[81,96,128]{2,1,0:T(8,128)(2,1)} %bitcast.35, bf16[2,4,1536]{2,1,0:T(4,128)(2,1)} %bitcast.40, ...), custom_call_target="tpu_custom_call" | custom-call | tf_op jit(solution)/shard_map/pallas_call | solution.py:262
  76.2 0.9 copy.13
  77.2 0.1 reshape.106
  77.3 1.0 slice_bitcast_fusion.1
  78.3 0.9 slice_bitcast_fusion.2
  79.2 0.8 slice_bitcast_fusion.4
  80.1 1.0 copy.14
  81.1 0.1 reshape.107
  81.2 0.1 add_convert_fusion
  81.3 0.1 maximum_select_fusion.1
  81.4 0.1 pad_dynamic-slice_fusion
  81.6 0.6 broadcast_in_dim_reshape.3
  82.2 0.0 copy-done
  82.2 8.8 %fusion.8 = bf16[1,4,8,52,384]{4,0,3,2,1:T(2,128)(2,1)S(1)} fusion(bf16[3,3,3,16,384]{4,3,2,1,0:T(8,128)(2,1)S(1)} %copy-done, bf16[1,6,10,54,16]{4,3,1,2,0:T(8,128)(2,1)S(1)} %broadcast_in_dim_reshape.3), kind=kOutput, calls=%fused_computation.13 | convolution fusion | flops 552075264 | bytes 1713408 | tf_op jit(solution)/shard_map/conv_general_dilated | solution.py:430
  91.0 0.0 copy-start.2
  91.0 0.4 fusion
  91.4 0.4 slice.38
  91.8 0.0 copy-done.2
  91.8 0.0 copy-start.1
  91.8 0.9 fusion.7
  92.7 0.2 pad.18.feat_ref
  92.9 0.0 copy-done.1
  92.9 1.4 %maximum_select_fusion = bf16[6,8,52,384]{3,2,1,0:T(8,128)(2,1)S(1)} fusion(bf16[4,8,52,384]{3,2,1,0:T(8,128)(2,1)S(1)} %fusion.7, bf16[2,8,2,384]{3,2,1,0:T(2,128)(2,1)S(1)} %fusion.12, bf16[2,2,48,384]{3,2,1,0:T(8,128)(2,1)S(1)} %get-tuple-element.18, bf16[2,4,48,384]{3,2,1,0:T(8,128)(2,1)S(1)} %bitcast.37, ...), kind=kLoop, calls=%fused_computation.11 | loop fusion | flops 12460032 | bytes 3809696 | tf_op jit(solution)/shard_map/jit(_where)/select_n | solution.py:442
  94.3 0.4 pad.17.x_ref
  94.7 35.4 %shard_map.92 = bf16[4,8,96,192]{3,2,1,0:T(8,128)(2,1)} custom-call(bf16[6,8,64,384]{3,2,1,0:T(8,128)(2,1)S(1)} %pad.17.x_ref, bf16[4,6,64,384]{3,2,1,0:T(8,128)(2,1)S(1)} %pad.18.feat_ref, f32[384,1]{1,0:T(8,128)S(1)} %reshape.114.mask_ref, bf16[81,384,128]{2,1,0:T(8,128)(2,1)} %bitcast.42, bf16[9,384,768]{2,1,0:T(8,128)(2,1)} %bitcast.43), custom_call_target="tpu_custom_call" | custom-call | flops 12230590464 | bytes 16777216 | tf_op jit(solution)/shard_map/pallas_call | solution.py:377
  (7 shorter events, 0.1 us)
Async XLA Ops:
  0.0 82.2 %copy-start = (bf16[3,3,3,16,384]{4,3,2,1,0:T(8,128)(2,1)S(1)}, bf16[3,3,3,16,384]{4,3,2,1,0:T(8,128)(2,1)}, u32[]{:S(2)}) copy-start(bf16[3,3,3,16,384]{4,3,2,1,0:T(8,128)(2,1)} %param.13) | copy-start | bytes 995332
  91.0 0.8 copy-start.2
  91.8 1.1 copy-start.1

commit v2 on v1

--- a/solution.py
+++ b/solution.py
@@ -9,6 +9,7 @@
 
 MESH = pl.DeviceIdType.MESH
 PIECES = 8
+PARTS = 2
 
 
 def exchange_kernel(
@@ -25,7 +26,8 @@
     o = 1 - s
     chunks = w_ref.shape[0]
     per = chunks // PIECES
-    half = per // 2
+    span = per // PARTS
+    half = span // 2
     rest = chunks - per * PIECES
     has = {-1: t > 0, 0: None, 1: t < n - 1}
 
@@ -54,7 +56,7 @@
             ),
         )
     own = [
-        pltpu.make_async_copy(w_ref, g_ref.at[:, t], own_sem.at[0]),
+        pltpu.make_async_copy(w_ref, g_ref.at[t], own_sem.at[0]),
         pltpu.make_async_copy(lat_ref, latx_ref.at[1, s], own_sem.at[1]),
         pltpu.make_async_copy(cl_ref, clx_ref.at[1, s], own_sem.at[2]),
     ]
@@ -112,94 +114,97 @@
             else:
                 events.append((i, d, t + 1 + i, t + 1 + i <= n - 1))
 
-    def block(group, part, u):
-        begin = (2 * (group % 4) + s) * per
+    def begin_of(group, q):
+        return (2 * (group % 4) + s) * per + q * span
+
+    def block(group, part, q, u):
+        begin = begin_of(group, q)
         if part == 0:
-            return g_ref.at[pl.ds(begin, half), u]
+            return g_ref.at[u, pl.ds(begin, half)]
         if part == 1:
-            return g_ref.at[pl.ds(begin + half, per - half), u]
-        return g_ref.at[pl.ds(begin, per), u]
+            return g_ref.at[u, pl.ds(begin + half, span - half)]
+        return g_ref.at[u, pl.ds(begin, span)]
 
     tail = pl.ds(per * PIECES, rest)
 
-    def z_copies(i, d, u, first):
-        begin = (2 * (g % 4) + s) * per
-        dt = 1 if d == 0 else -1
-        e = 2 * i + d
-        src_a = w_ref.at[pl.ds(begin, per)] if first else block(g, 2, u)
-        src_b = w_ref.at[tail] if first else g_ref.at[tail, u]
-        target = dev(0, None, dt)
-        return [
-            remote(src_a, block(g, 2, u), zs_sem.at[2 * e], zr_sem.at[2 * e], target),
-            remote(src_b, g_ref.at[tail, u], zs_sem.at[2 * e + 1], zr_sem.at[2 * e + 1], target),
-        ]
-
-    def d_copies(e, u):
+    def z_copies(i, d, q, u, first):
+        e = (2 * i + d) * PARTS + q
+        target = dev(0, None, 1 if d == 0 else -1)
+        src = w_ref.at[pl.ds(begin_of(g, q), span)] if first else block(g, 2, q, u)
+        made = [remote(src, block(g, 2, q, u), zs_sem.at[2 * e], zr_sem.at[2 * e], target)]
+        if q == PARTS - 1 and rest:
+            src = w_ref.at[tail] if first else g_ref.at[u, tail]
+            k = 2 * e + 1
+            made.append(remote(src, g_ref.at[u, tail], zs_sem.at[k], zr_sem.at[k], target))
+        return made
+
+    def d_copies(e, q, u):
         def one(k, group, part, to):
-            b = block(group, part, u)
+            b = block(group, part, q, u)
             return remote(b, b, ps_sem.at[6 * e + k], pr_sem.at[6 * e + k], dev(0, to))
 
         first = [one(0, g, 0, gx), one(1, g, 1, gy)]
         second = [one(2, g, 0, gy), one(3, gx, 0, gy), one(4, g, 1, gx), one(5, gy, 1, gx)]
         return first, second
 
-    def s_copies(e, u):
+    def s_copies(e, q, u):
         plan = [(g, 2), (gx, 0), (gy, 1), (gy, 0), (gd, 0), (gx, 1), (gd, 1)]
         made = []
         for k, (group, part) in enumerate(plan):
-            b = block(group, part, u)
+            b = block(group, part, q, u)
             made.append(remote(b, b, ss_sem.at[7 * e + k], sr_sem.at[7 * e + k], dev(1)))
         return made
 
-    def begin_z(i, d, u, valid, first):
+    def begin_z(i, d, q, u, valid, first):
         dt = 1 if d == 0 else -1
 
         def go():
-            for copy in z_copies(i, d, u, first):
+            for copy in z_copies(i, d, q, u, first):
                 copy.start()
 
         pl.when(jnp.logical_and(valid, has[dt]))(go)
 
-    def end_z(i, d, u, valid):
+    def end_z(i, d, q, u, valid):
         dt = 1 if d == 0 else -1
 
         def go():
-            for copy in z_copies(i, d, u, i == 0):
+            for copy in z_copies(i, d, q, u, i == 0):
                 copy.wait_send()
 
         pl.when(jnp.logical_and(valid, has[dt]))(go)
 
-    begin_z(0, 0, t, t >= 0, True)
-    begin_z(0, 1, t, t >= 0, True)
+    for q in range(PARTS):
+        begin_z(0, 0, q, t, t >= 0, True)
+        begin_z(0, 1, q, t, t >= 0, True)
     for dt, ds, copies in halo:
         def go(copies=copies):
             for copy in copies:
                 copy.start()
         guarded(has[dt], go)
 
-    def arrive(e, i, d, u):
-        for copy in z_copies(i, d, u, False):
+    def arrive(i, d, q, u):
+        for copy in z_copies(i, d, q, u, False):
             copy.wait_recv()
 
-    def stage_a(i, d, u, valid):
-        e = 2 * i + d
+    def stage_a(i, d, q, u, valid):
+        e = (2 * i + d) * PARTS + q
 
         def go():
-            arrive(e, i, d, u)
-            for copy in d_copies(e, u)[0]:
+            arrive(i, d, q, u)
+            if i + 1 < n - 1:
+                begin_z(i + 1, d, q, u, valid, False)
+            for copy in d_copies(e, q, u)[0]:
                 copy.start()
-            s_copies(e, u)[0].start()
+            s_copies(e, q, u)[0].start()
 
         pl.when(valid)(go)
-        if i + 1 < n - 1:
-            begin_z(i + 1, d, u, valid, False)
-
-    def stage_b(i, d, u, valid):
-        e = 2 * i + d
+
+    def stage_b(i, d, q, u, valid):
+        e = (2 * i + d) * PARTS + q
 
         def go():
-            first, second = d_copies(e, u)
-            sib = s_copies(e, u)
+            first, second = d_copies(e, q, u)
+            sib = s_copies(e, q, u)
             first[0].wait_recv()
             second[0].start()
             second[1].start()
@@ -211,24 +216,24 @@
 
         pl.when(valid)(go)
 
-    def stage_c(i, d, u, valid):
-        e = 2 * i + d
+    def stage_c(i, d, q, u, valid):
+        e = (2 * i + d) * PARTS + q
 
         def go():
-            _, second = d_copies(e, u)
-            sib = s_copies(e, u)
+            _, second = d_copies(e, q, u)
+            sib = s_copies(e, q, u)
             for k in range(4):
                 second[k].wait_recv()
                 sib[3 + k].start()
 
         pl.when(valid)(go)
 
-    for slot in range(n + 1):
+    for slot in range((n - 1) * PARTS + 2):
         for stage, lag in ((stage_a, 0), (stage_b, 1), (stage_c, 2)):
-            i = slot - lag
+            i, q = (slot - lag) // PARTS, (slot - lag) % PARTS
             if 0 <= i < n - 1:
-                for event in events[2 * i : 2 * i + 2]:
-                    stage(*event)
+                for _, d, u, valid in events[2 * i : 2 * i + 2]:
+                    stage(i, d, q, u, valid)
 
     for copy in own:
         copy.wait()
@@ -238,31 +243,31 @@
     for (dt, ds), copies in order.items():
         guarded(has[-dt], lambda copies=copies: [c.wait_recv() for c in copies] and None)
     for i, d, u, valid in events:
-        e = 2 * i + d
-
-        def finish(e=e, u=u):
-            first, second = d_copies(e, u)
-            for copy in first + second:
-                copy.wait_send()
-            for copy in s_copies(e, u):
-                copy.wait()
-
-        pl.when(valid)(finish)
-        sent = t - i if d == 0 else t + i
-        end_z(i, d, sent, sent >= 0 if d == 0 else sent <= n - 1)
+        for q in range(PARTS):
+            e = (2 * i + d) * PARTS + q
+
+            def finish(e=e, q=q, u=u):
+                first, second = d_copies(e, q, u)
+                for copy in first + second:
+                    copy.wait_send()
+                for copy in s_copies(e, q, u):
+                    copy.wait()
+
+            pl.when(valid)(finish)
+            sent = t - i if d == 0 else t + i
+            end_z(i, d, q, sent, sent >= 0 if d == 0 else sent <= n - 1)
 
 
 def exchange(n, weights, latent, cache_latent, mid_cache):
-    chunks, cw, lanes = weights.shape
     frames, rows, cols, channels = mid_cache.shape
     dt = weights.dtype
     shape = jax.ShapeDtypeStruct
-    events = 2 * (n - 1)
+    events = 2 * (n - 1) * PARTS
     dma = lambda k: pltpu.SemaphoreType.DMA((k,))
     return pl.pallas_call(
         functools.partial(exchange_kernel, n),
         out_shape=(
-            shape((chunks, n, cw, lanes), dt),
+            shape((n,) + weights.shape, dt),
             shape((3, 2) + latent.shape, dt),
             shape((3, 2) + cache_latent.shape, dt),
             shape((2, frames, 2, cols, channels), dt),
@@ -298,7 +303,6 @@
     rows = inner - 2
     cols = out_ref.shape[2] // 2
     out_channels = out_ref.shape[3]
-    pair = 2
 
     @pl.when(step == 0)
     def _():
@@ -314,16 +318,18 @@
     @pl.when(step < 9)
     def _():
         a, b = step // 3, step % 3
-        for c in range(3):
-            weights = jnp.concatenate([w_ref[3 * c + k] for k in range(3)], axis=1)
-            for p in range(frames // pair):
-                where = (pl.ds(a + pair * p, pair), pl.ds(b, inner))
-                left = x_ref[where] if c == 0 else xs_ref[(c - 1,) + where]
-                size = pair * inner * wide
-                acc_ref[p * size : (p + 1) * size] += lax.dot_general(
-                    left.reshape(size, mid), weights, (((1,), (1,)), ((), ())),
-                    preferred_element_type=jnp.float32,
-                )
+        where = (pl.ds(a, frames), pl.ds(b, inner))
+        size = frames * inner * wide
+        left = [x_ref[where]] + [xs_ref[(c,) + where] for c in range(2)]
+        left = jnp.concatenate([v.reshape(size, mid) for v in left], axis=1)
+        weights = [
+            jnp.concatenate([w_ref[u, c] for u in range(w_ref.shape[0])], axis=0)
+            for c in range(3)
+        ]
+        acc_ref[...] += lax.dot_general(
+            left, jnp.concatenate(weights, axis=1), (((1,), (1,)), ((), ())),
+            preferred_element_type=jnp.float32,
+        )
 
     @pl.when(step == 9)
     def _():
@@ -342,13 +348,12 @@
     @pl.when(step >= 9)
     def _():
         b = step - 9
-        for c in range(3):
-            for p in range(frames // pair):
-                left = mx_ref[c, pl.ds(pair * p, pair), pl.ds(b, rows), pl.ds(0, cols)]
-                size = pair * rows * cols
-                up_ref[p * size : (p + 1) * size] += jnp.dot(
-                    left.reshape(size, mid), u_ref[c], preferred_element_type=jnp.float32
-                )
+        size = frames * rows * cols
+        left = [mx_ref[c, :, pl.ds(b, rows), pl.ds(0, cols)] for c in range(3)]
+        left = jnp.concatenate([v.reshape(size, mid) for v in left], axis=1)
+        up_ref[...] += jnp.dot(
+            left, u_ref[...].reshape(3 * mid, u_ref.shape[2]), preferred_element_type=jnp.float32
+        )
 
     @pl.when(step == 11)
     def _():
@@ -382,7 +387,10 @@
             whole,
             whole,
             whole,
-            pl.BlockSpec((9, mid, weights.shape[2]), lambda i: (jnp.minimum(i, 8), 0, 0)),
+            pl.BlockSpec(
+                (weights.shape[0], 3) + weights.shape[2:],
+                lambda i: (0, jnp.minimum(i, 8), 0, 0),
+            ),
             pl.BlockSpec((3, mid, phases), lambda i: (jnp.maximum(i - 9, 0), 0, 0)),
         ],
         out_specs=whole,
@@ -407,9 +415,8 @@
     channels = latent_mean.shape[0]
     mid = input_weight.shape[-1]
     cw = mid_weight.shape[-1]
-    lanes = 128
     _, rows, cols, _ = mid_cache.shape[1:]
-    shard = mid_weight.reshape(-1, lanes, cw).transpose(0, 2, 1)
+    shard = mid_weight.transpose(0, 1, 2, 4, 3).reshape(-1, 16 if cw % 16 == 0 else 8, mid)
     gathered, latx, clx, mcv, mch = exchange(
         n, shard, latent[0], cache_latent[0], mid_cache[0]
     )
@@ -446,7 +453,7 @@
     keep = jnp.logical_and(row_ok, col_ok)[1:-1, 1:]
     keep = jnp.pad(keep, ((0, 0), (0, wide - cols - 3), (0, 0))).astype(jnp.float32)
     out = convs(
-        stacked, inner, keep.reshape(-1, 1), gathered.reshape(gathered.shape[0], mid, lanes),
+        stacked, inner, keep.reshape(-1, 1), gathered.reshape(n, 27, cw, mid),
         up_weight.reshape((9,) + up_weight.shape[2:]), cols,
     )
     return out[None]

time: 131 us -> 120 us (0.916)
  local copies, waits for them, and re-layouts: 17.9 us -> 8.31 us
    reshape x2 -> x0, local copies, waits for them, and re-layouts: 6.7 us -> none  [local(): shard = mid_weight.reshape(-1, lanes, cw).transpose(0, 2, 1)]
    pallas_call x1, Pallas kernels: 35.4 us -> 32.5 us  [convs(): pl.pallas_call(convs_kernel, grid=(12,), out_shape=jax.ShapeDtypeStruct((...]
    unnamed x7 -> x6, local copies, waits for them, and re-layouts: 2.94 us -> 0.02 us
    pallas_call x1, Pallas kernels: 64.7 us -> 66.6 us  [exchange(): pl.pallas_call(functools.partial(exchange_kernel, n), out_shape=(shape((n...]
where the time goes in v2:
time: 120 us; the launch traced here: 119 us
  Pallas kernels  99 us (82%)
  matrix products  8.8 us (7%)
  local copies, waits for them, and re-layouts  8.31 us (7%)
  other arithmetic  3.13 us (3%)
    pallas_call x1, Pallas kernels, exchange(): pl.pallas_call(functools.partial(exchange_kernel, n), out_shape=(shape((n...  66.6 us
    pallas_call x1, Pallas kernels, convs(): pl.pallas_call(convs_kernel, grid=(12,), out_shape=jax.ShapeDtypeStruct((...  32.5 us
    conv_general_dilated x1, matrix products, local(): lax.conv_general_dilated(joined[None], input_weight, (1, 1, 1), [(0, 0)]...  8.8 us

profile of v2, /device:TPU:12, one launch (start us, length us, event | category | flops | bytes accessed | tf_op | source)
XLA Modules:
  0.0 119.5 jit_solution(5722803188768292785)
XLA Ops:
  0.0 0.0 copy-start
  0.0 0.1 broadcast_and_fusion
  0.1 0.1 broadcast_and_fusion.1
  0.2 0.1 slice.35
  0.3 0.7 tile.5
  0.9 0.1 add.73
  1.0 0.7 tile.4
  1.7 0.1 mul.46
  1.8 0.2 reshape.114.mask_ref
  1.9 66.6 %shard_map.91 = (bf16[4,162,16,384]{3,2,1,0:T(8,128)(2,1)}, bf16[3,2,2,4,1536]{4,3,2,1,0:T(4,128)(2,1)}, bf16[3,2,2,4,768]{4,3,2,1,0:T(4,128)(2,1)}, bf16[2,2,2,...) custom-call(bf16[162,16,384]{2,1,0:T(8,128)(2,1)} %bitcast.33, bf16[2,4,1536]{2,1,0:T(4,128)(2,1)} %bitcast.38, ...), custom_call_target="tpu_custom_call" | custom-call | tf_op jit(solution)/shard_map/pallas_call | solution.py:267
  68.5 0.9 copy.11
  69.4 0.1 reshape.106
  69.6 1.0 slice_bitcast_fusion.1
  70.6 0.9 slice_bitcast_fusion.2
  71.5 0.8 slice_bitcast_fusion.4
  72.4 1.0 copy.12
  73.4 0.1 reshape.107
  73.5 0.1 add_convert_fusion
  73.5 0.1 maximum_select_fusion.1
  73.7 0.1 pad_dynamic-slice_fusion
  73.8 0.6 broadcast_in_dim_reshape.3
  74.4 0.0 copy-done
  74.5 8.8 %fusion.8 = bf16[1,4,8,52,384]{4,0,3,2,1:T(2,128)(2,1)S(1)} fusion(bf16[3,3,3,16,384]{4,3,2,1,0:T(8,128)(2,1)S(1)} %copy-done, bf16[1,6,10,54,16]{4,3,1,2,0:T(8,128)(2,1)S(1)} %broadcast_in_dim_reshape.3), kind=kOutput, calls=%fused_computation.12 | convolution fusion | flops 552075264 | bytes 1713408 | tf_op jit(solution)/shard_map/conv_general_dilated | solution.py:437
  83.3 0.0 copy-start.2
  83.3 0.4 fusion
  83.7 0.4 slice.38
  84.1 0.0 copy-done.2
  84.1 0.0 copy-start.1
  84.1 0.9 fusion.7
  85.0 0.2 pad.18.feat_ref
  85.1 0.0 copy-done.1
  85.2 1.4 %maximum_select_fusion = bf16[6,8,52,384]{3,2,1,0:T(8,128)(2,1)S(1)} fusion(bf16[4,8,52,384]{3,2,1,0:T(8,128)(2,1)S(1)} %fusion.7, bf16[2,8,2,384]{3,2,1,0:T(2,128)(2,1)S(1)} %fusion.12, bf16[2,2,48,384]{3,2,1,0:T(8,128)(2,1)S(1)} %get-tuple-element.18, bf16[2,4,48,384]{3,2,1,0:T(8,128)(2,1)S(1)} %bitcast.35, ...), kind=kLoop, calls=%fused_computation.11 | loop fusion | flops 12460032 | bytes 3809696 | tf_op jit(solution)/shard_map/jit(_where)/select_n | solution.py:449
  86.6 0.4 pad.17.x_ref
  87.0 32.5 %shard_map.92 = bf16[4,8,96,192]{3,2,1,0:T(8,128)(2,1)} custom-call(bf16[6,8,64,384]{3,2,1,0:T(8,128)(2,1)S(1)} %pad.17.x_ref, bf16[4,6,64,384]{3,2,1,0:T(8,128)(2,1)S(1)} %pad.18.feat_ref, f32[384,1]{1,0:T(8,128)S(1)} %reshape.114.mask_ref, bf16[4,27,96,384]{3,2,1,0:T(8,128)(2,1)} %bitcast.40, bf16[9,384,768]{2,1,0:T(8,128)(2,1)} %bitcast.41), custom_call_target="tpu_custom_call" | custom-call | flops 12230590464 | bytes 16777216 | tf_op jit(solution)/shard_map/pallas_call | solution.py:382
  (7 shorter events, 0.1 us)
Async XLA Ops:
  0.0 74.4 %copy-start = (bf16[3,3,3,16,384]{4,3,2,1,0:T(8,128)(2,1)S(1)}, bf16[3,3,3,16,384]{4,3,2,1,0:T(8,128)(2,1)}, u32[]{:S(2)}) copy-start(bf16[3,3,3,16,384]{4,3,2,1,0:T(8,128)(2,1)} %param.13) | copy-start | bytes 995332
  83.3 0.8 copy-start.2
  84.1 1.1 copy-start.1

commit v3 on v2

--- a/solution.py
+++ b/solution.py
@@ -283,19 +283,14 @@
     )(weights, latent, cache_latent, mid_cache)
 
 
-def activate(values, gain_vector):
-    floats = values.astype(jnp.float32)
-    inverse_rms = lax.rsqrt(jnp.mean(floats * floats, axis=-1, keepdims=True) + 1e-06)
-    return jax.nn.silu(floats * inverse_rms * gain_vector).astype(jnp.bfloat16)
-
-
 def inside(start, count, limit):
     index = start + jnp.arange(count)
     return jnp.logical_and(index >= 0, index < limit)
 
 
 def convs_kernel(
-    x_ref, feat_ref, mask_ref, w_ref, u_ref, out_ref, xs_ref, acc_ref, mx_ref, up_ref, tmp_ref
+    beside_ref, taps_ref, gain_ref, cache_ref, region_ref, mask_ref, w_ref, u_ref, out_ref,
+    x_ref, feat_ref, xs_ref, acc_ref, mx_ref, up_ref, tmp_ref,
 ):
     step = pl.program_id(0)
     total, tall, wide, mid = x_ref.shape
@@ -307,6 +302,25 @@
     @pl.when(step == 0)
     def _():
         acc_ref[...] = jnp.zeros_like(acc_ref)
+        x_ref[0 : total - frames] = cache_ref[...]
+        size = tall * wide
+
+        @pl.loop(0, frames)
+        def _(f):
+            value = jnp.zeros((size, mid), jnp.float32)
+            for a in range(3):
+                for b in range(3):
+                    left = beside_ref[f + a, b : b + tall].reshape(size, beside_ref.shape[3])
+                    value += jnp.dot(
+                        left, taps_ref[3 * a + b], preferred_element_type=jnp.float32
+                    )
+            value = value.astype(jnp.bfloat16).astype(jnp.float32)
+            moved = pltpu.roll(value, size - 1, axis=0).reshape(tall, wide, mid)
+            feat_ref[f] = moved[1:-1].astype(jnp.bfloat16)
+            power = jnp.mean(value * value, axis=-1, keepdims=True)
+            value = value * lax.rsqrt(power + 1e-06) * gain_ref[...]
+            value = jnp.where(region_ref[...] > 0, value / (1.0 + jnp.exp(-value)), 0.0)
+            x_ref[total - frames + f] = value.astype(jnp.bfloat16).reshape(tall, wide, mid)
 
         @pl.loop(0, total)
         def _(f):
@@ -372,8 +386,9 @@
                 out_ref[f, 2 * r + i] = joined[:, :out_channels].astype(jnp.bfloat16)
 
 
-def convs(stacked, features, mask, weights, up_weight, cols):
-    total, tall, wide, mid = stacked.shape
+def convs(beside, taps, gain, cache, region, mask, weights, up_weight, cols):
+    total = beside.shape[0]
+    tall, wide, mid = cache.shape[1:]
     frames, inner = total - 2, tall - 2
     rows = inner - 2
     phases = up_weight.shape[-1]
@@ -387,6 +402,9 @@
             whole,
             whole,
             whole,
+            whole,
+            whole,
+            whole,
             pl.BlockSpec(
                 (weights.shape[0], 3) + weights.shape[2:],
                 lambda i: (0, jnp.minimum(i, 8), 0, 0),
@@ -395,6 +413,8 @@
         ],
         out_specs=whole,
         scratch_shapes=[
+            pltpu.VMEM((total, tall, wide, mid), jnp.bfloat16),
+            pltpu.VMEM((frames, inner, wide, mid), jnp.bfloat16),
             pltpu.VMEM((2, total, tall, wide, mid), jnp.bfloat16),
             pltpu.VMEM((frames * inner * wide, mid), jnp.float32),
             pltpu.VMEM((3, frames, inner, wide, mid), jnp.bfloat16),
@@ -403,7 +423,7 @@
         ],
         compiler_params=pltpu.CompilerParams(vmem_limit_bytes=48 * 2**20),
         cost_estimate=pl.CostEstimate(flops=flops, bytes_accessed=16 * 2**20, transcendentals=0),
-    )(stacked, features, mask, weights, up_weight)
+    )(beside, taps, gain, cache, region, mask, weights, up_weight)
 
 
 def local(
@@ -434,26 +454,23 @@
     joined = jnp.pad(joined, ((0, 0), (0, 0), (3 * channels, 3 * channels)))
     joined = lax.dynamic_slice_in_dim(joined, s * cols * channels, (cols + 6) * channels, axis=2)
     joined = joined.reshape(joined.shape[0], rows + 6, cols + 6, channels)
-    features = lax.conv_general_dilated(
-        joined[None], input_weight, (1, 1, 1), [(0, 0)] * 3,
-        dimension_numbers=("NDHWC", "DHWIO", "NDHWC"),
-        preferred_element_type=jnp.float32,
-    )[0].astype(jnp.bfloat16)
+    wide = -(-(cols + 4) // 16) * 16
+    extra = wide - cols - 4
+    beside = jnp.concatenate([joined[:, :, c : c + cols + 4] for c in range(3)], axis=-1)
+    beside = jnp.pad(beside, ((0, 0), (0, 0), (0, extra), (0, 0)))
     sided = jnp.concatenate([mch[0, :, :2], mch[1], mch[2, :, :2]], axis=1)
     sided = lax.dynamic_slice_in_dim(sided, 14 * s, 2, axis=2)
     centre = jnp.concatenate([mcv[0], mid_cache[0], mcv[1]], axis=1)
     cache = jnp.concatenate([sided, centre, sided], axis=2)
-    stacked = jnp.concatenate([cache, activate(features, mid_gain)], axis=0)
     row_ok = inside(t * rows - 2, rows + 4, n * rows)[:, None, None]
     col_ok = inside(s * cols - 2, cols + 4, 2 * cols)[:, None]
-    stacked = jnp.where(jnp.logical_and(row_ok, col_ok), stacked, 0)
-    wide = -(-(cols + 4) // 16) * 16
-    stacked = jnp.pad(stacked, ((0, 0), (0, 0), (0, wide - cols - 4), (0, 0)))
-    inner = jnp.pad(features[:, 1:-1, 1:], ((0, 0), (0, 0), (0, wide - cols - 3), (0, 0)))
-    keep = jnp.logical_and(row_ok, col_ok)[1:-1, 1:]
-    keep = jnp.pad(keep, ((0, 0), (0, wide - cols - 3), (0, 0))).astype(jnp.float32)
+    region = jnp.logical_and(row_ok, col_ok)
+    cache = jnp.pad(jnp.where(region, cache, 0), ((0, 0), (0, 0), (0, extra), (0, 0)))
+    keep = jnp.pad(region[1:-1, 1:], ((0, 0), (0, extra + 1), (0, 0))).astype(jnp.float32)
+    region = jnp.pad(region, ((0, 0), (0, extra), (0, 0))).astype(jnp.float32)
     out = convs(
-        stacked, inner, keep.reshape(-1, 1), gathered.reshape(n, 27, cw, mid),
+        beside, input_weight.reshape(9, 3 * channels, mid), mid_gain[None], cache,
+        region.reshape(-1, 1), keep.reshape(-1, 1), gathered.reshape(n, 27, cw, mid),
         up_weight.reshape((9,) + up_weight.shape[2:]), cols,
     )
     return out[None]

time: 120 us -> 112 us (0.933)
  matrix products: 8.8 us -> 0 us
  Pallas kernels: 99 us -> 104 us
  local copies, waits for them, and re-layouts: 8.31 us -> 5.06 us
  other arithmetic: 3.13 us -> 1.62 us
    conv_general_dilated x1 -> x0, matrix products: 8.8 us -> none  [local(): lax.conv_general_dilated(joined[None], input_weight, (1, 1, 1), [(0, 0)]...]
    pallas_call x1, Pallas kernels: 32.5 us -> 37.9 us  [convs(): pl.pallas_call(convs_kernel, grid=(12,), out_shape=jax.ShapeDtypeStruct((...]
    squeeze x2, local copies, waits for them, and re-layouts: 1.75 us -> 0.02 us  [local(): sided = jnp.concatenate([mch[0, :, :2], mch[1], mch[2, :, :2]], axis=1)]
where the time goes in v3:
time: 112 us; the launch traced here: 111 us
  Pallas kernels  104 us (93%)
  local copies, waits for them, and re-layouts  5.06 us (5%)
  other arithmetic  1.62 us (1%)
    pallas_call x1, Pallas kernels, exchange(): pl.pallas_call(functools.partial(exchange_kernel, n), out_shape=(shape((n...  66.5 us
    pallas_call x1, Pallas kernels, convs(): pl.pallas_call(convs_kernel, grid=(12,), out_shape=jax.ShapeDtypeStruct((...  37.9 us

profile of v3, /device:TPU:12, one launch (start us, length us, event | category | flops | bytes accessed | tf_op | source)
XLA Modules:
  0.0 111.4 jit_solution(14213671132822894758)
XLA Ops:
  0.0 0.0 copy-start.5
  0.0 0.0 copy-start.6
  0.0 66.5 %shard_map.91 = (bf16[4,162,16,384]{3,2,1,0:T(8,128)(2,1)}, bf16[3,2,2,4,1536]{4,3,2,1,0:T(4,128)(2,1)}, bf16[3,2,2,4,768]{4,3,2,1,0:T(4,128)(2,1)}, bf16[2,2,2,...) custom-call(bf16[162,16,384]{2,1,0:T(8,128)(2,1)} %bitcast.33, bf16[2,4,1536]{2,1,0:T(4,128)(2,1)} %bitcast.38, ...), custom_call_target="tpu_custom_call" | custom-call | tf_op jit(solution)/shard_map/pallas_call | solution.py:267
  66.5 1.0 copy.11
  67.5 0.1 reshape.108
  67.6 0.0 copy-done.5
  67.6 0.1 add.53
  67.7 0.0 copy-done.6
  67.7 0.1 mul.22
  67.8 0.1 add_convert_fusion
  67.9 0.9 copy.10
  68.8 0.1 reshape.107
  68.9 0.1 maximum_select_fusion.1
  69.1 0.1 pad_dynamic-slice_fusion
  69.2 0.6 reshape.109
  69.8 0.5 fusion.2
  70.3 0.8 pad_maximum_fusion
  71.1 0.0 copy-start.3
  71.2 0.1 copy.20
  71.2 0.0 copy-start.2
  71.2 0.0 copy-start.1
  71.3 0.3 pad.21.beside_ref
  71.5 0.6 copy-done.3
  72.2 0.1 broadcast_and_fusion.1
  72.3 0.0 copy-done.2
  72.3 0.0 copy-done.1
  72.3 0.0 copy-start.4
  72.4 0.0 copy-start
  72.4 0.4 maximum_select_fusion
  72.7 0.1 pad.22.cache_ref
  72.9 0.1 broadcast_and_fusion
  72.9 0.2 reshape.121.region_ref
  73.1 0.1 slice.43
  73.2 0.2 reshape.122.mask_ref
  73.4 0.0 copy-done.4
  73.4 0.0 copy-done
  73.4 37.9 %shard_map.92 = bf16[4,8,96,192]{3,2,1,0:T(8,128)(2,1)} custom-call(bf16[6,10,64,48]{3,2,1,0:T(8,128)(2,1)S(1)} %pad.21.beside_ref, bf16[9,48,384]{2,1,0:T(8,128)(2,1)S(1)} %bitcast.32, f32[1,384]{1,0:T(1,128)S(1)} %broadcast_in_dim.34.gain_ref, bf16[2,8,64,384]{3,2,1,0:T(8,128)(2,1)S(1)} %pad.22.cache_ref, f32[512,1]{1,0:T(8,128)S(1)} %reshape.121.region_ref, ...), custom_call_target="tpu_custom_call" | custom-call | flops 12230590464 | bytes 16777216 | tf_op jit(solution)/shard_map/pallas_call | solution.py:397
  (13 shorter events, 0.2 us)
Async XLA Ops:
  0.0 67.6 %copy-start.5 = (f32[16]{0:T(128)S(1)}, f32[16]{0:T(128)}, u32[]{:S(2)}) copy-start(f32[16]{0:T(128)} %param.10) | copy-start | bytes 196
  0.0 67.7 %copy-start.6 = (f32[16]{0:T(128)S(1)}, f32[16]{0:T(128)}, u32[]{:S(2)}) copy-start(f32[16]{0:T(128)} %param.11) | copy-start | bytes 196
  71.1 1.0 copy-start.3
  71.2 1.1 copy-start.2
  71.2 1.1 copy-start.1
  72.3 1.1 copy-start.4
  72.4 1.1 copy-start

commit v4 on v3

--- a/solution.py
+++ b/solution.py
@@ -9,7 +9,7 @@
 
 MESH = pl.DeviceIdType.MESH
 PIECES = 8
-PARTS = 2
+PARTS = 1
 
 
 def exchange_kernel(

time: 112 us -> 110 us (0.982)
    pallas_call x1, Pallas kernels: 66.5 us -> 64.7 us  [exchange(): pl.pallas_call(functools.partial(exchange_kernel, n), out_shape=(shape((n...]
where the time goes in v4:
time: 110 us
  Pallas kernels  103 us (94%)
  local copies, waits for them, and re-layouts  5.06 us (5%)
  other arithmetic  1.62 us (1%)
    pallas_call x1, Pallas kernels, exchange(): pl.pallas_call(functools.partial(exchange_kernel, n), out_shape=(shape((n...  64.7 us
    pallas_call x1, Pallas kernels, convs(): pl.pallas_call(convs_kernel, grid=(12,), out_shape=jax.ShapeDtypeStruct((...  37.9 us

profile of v4, /device:TPU:12, one launch (start us, length us, event | category | flops | bytes accessed | tf_op | source)
XLA Modules:
  0.0 109.6 jit_solution(6989221565366807787)
XLA Ops:
  0.0 0.0 copy-start.5
  0.0 0.0 copy-start.6
  0.0 64.7 %shard_map.91 = (bf16[4,162,16,384]{3,2,1,0:T(8,128)(2,1)}, bf16[3,2,2,4,1536]{4,3,2,1,0:T(4,128)(2,1)}, bf16[3,2,2,4,768]{4,3,2,1,0:T(4,128)(2,1)}, bf16[2,2,2,...) custom-call(bf16[162,16,384]{2,1,0:T(8,128)(2,1)} %bitcast.33, bf16[2,4,1536]{2,1,0:T(4,128)(2,1)} %bitcast.38, ...), custom_call_target="tpu_custom_call" | custom-call | tf_op jit(solution)/shard_map/pallas_call | solution.py:267
  64.7 1.0 copy.11
  65.7 0.1 reshape.108
  65.8 0.0 copy-done.5
  65.8 0.1 add.53
  65.9 0.0 copy-done.6
  65.9 0.1 mul.22
  66.0 0.1 add_convert_fusion
  66.1 0.9 copy.10
  67.0 0.1 reshape.107
  67.1 0.1 maximum_select_fusion.1
  67.3 0.1 pad_dynamic-slice_fusion
  67.4 0.6 reshape.109
  68.1 0.5 fusion.2
  68.5 0.8 pad_maximum_fusion
  69.3 0.0 copy-start.3
  69.4 0.1 copy.20
  69.4 0.0 copy-start.2
  69.4 0.0 copy-start.1
  69.5 0.3 pad.21.beside_ref
  69.7 0.6 copy-done.3
  70.4 0.1 broadcast_and_fusion.1
  70.5 0.0 copy-done.2
  70.5 0.0 copy-done.1
  70.6 0.0 copy-start.4
  70.6 0.0 copy-start
  70.6 0.4 maximum_select_fusion
  70.9 0.1 pad.22.cache_ref
  71.1 0.1 broadcast_and_fusion
  71.1 0.2 reshape.121.region_ref
  71.3 0.1 slice.43
  71.4 0.2 reshape.122.mask_ref
  71.6 0.0 copy-done.4
  71.6 0.0 copy-done
  71.6 37.9 %shard_map.92 = bf16[4,8,96,192]{3,2,1,0:T(8,128)(2,1)} custom-call(bf16[6,10,64,48]{3,2,1,0:T(8,128)(2,1)S(1)} %pad.21.beside_ref, bf16[9,48,384]{2,1,0:T(8,128)(2,1)S(1)} %bitcast.32, f32[1,384]{1,0:T(1,128)S(1)} %broadcast_in_dim.34.gain_ref, bf16[2,8,64,384]{3,2,1,0:T(8,128)(2,1)S(1)} %pad.22.cache_ref, f32[512,1]{1,0:T(8,128)S(1)} %reshape.121.region_ref, ...), custom_call_target="tpu_custom_call" | custom-call | flops 12230590464 | bytes 16777216 | tf_op jit(solution)/shard_map/pallas_call | solution.py:397
  (13 shorter events, 0.2 us)
Async XLA Ops:
  0.0 65.8 %copy-start.5 = (f32[16]{0:T(128)S(1)}, f32[16]{0:T(128)}, u32[]{:S(2)}) copy-start(f32[16]{0:T(128)} %param.10) | copy-start | bytes 196
  0.0 65.9 %copy-start.6 = (f32[16]{0:T(128)S(1)}, f32[16]{0:T(128)}, u32[]{:S(2)}) copy-start(f32[16]{0:T(128)} %param.11) | copy-start | bytes 196
  69.3 1.0 copy-start.3
  69.4 1.1 copy-start.2
  69.4 1.1 %copy-start.1 = (bf16[1,2,4,48,384]{4,3,2,1,0:T(8,128)(2,1)S(1)}, bf16[1,2,4,48,384]{4,3,2,1,0:T(8,128)(2,1)}, u32[]{:S(2)}) copy-start(bf16[1,2,4,48,384]{4,3,2,1,0:T(8,128)(2,1)} %param.15) | copy-start | bytes 884740
  70.6 1.1 copy-start.4
  70.6 1.1 copy-start
